TPU v7x, 32 devices: a whole 2x2x4 slice. The times are simulated.
32 devices in a mesh: groups: 2 (over y), gx: 4 (over z), gz: 2 (over x), vert: 2 (over core).
Axes of the slice: x: 2, y: 2, z: 4, core: 2. Of those that a mesh axis runs over, the one named last changes fastest.
Arguments:
- flow_field: bfloat16 [4, 4, 5, 4, 256, 256], P('groups', 'vert', None, 'gx', None, 'gz'), parts along dimension 0, may hold values from -6 to 6
- test_streams: int32 [4], P('groups'), parts along dimension 0, may hold values from 0 to 999999
- snapshot_ids: int32 [4, 4], P('groups', 'vert'), parts along dimension 0, may hold values from 0 to 65535
Outputs:
- sketch_x: float32 [8, 128], P(('groups', 'gx')), parts along dimension 0
- sketch_y: float32 [512, 128], P(('groups', 'gx', 'gz', 'vert')), parts along dimension 0
- sketch_z: float32 [512, 128], P(('groups', 'gz'), ('gx', 'vert')), parts along dimension 0
- core_sketch: float32 [4608, 2, 48], P(('groups', 'gx')), parts along dimension 0
There are 2 independent parts, one for each index of `groups`. A program takes and returns all parts, laid end to end along the dimension named above; each array names one. Nothing has to cross between parts.
All inputs are finite; a program needn't handle non-finite values.
Results may differ from a plain program's by a relative error of at most 0.007.
Values sent between devices are 32-bit elements; how exact they have to be, the bound alone decides.
A program may use at most 64 MiB of HBM per device.

v0:
```python
import functools
import math

import jax
import jax.numpy as jnp
from jax import lax
from jax.experimental import pallas as pl
from jax.experimental.pallas import tpu as pltpu
from jax.sharding import PartitionSpec as P

K = 128
S = 48
E = 2


def hash_index(index, stream, salt):
    mixed = index * -1640531535 + stream * -2048144777 + salt
    mixed = jnp.bitwise_xor(mixed, lax.shift_right_logical(mixed, jnp.int32(16)))
    mixed = mixed * 739982445
    mixed = jnp.bitwise_xor(mixed, lax.shift_right_logical(mixed, jnp.int32(13)))
    mixed = mixed * 695872825
    return jnp.bitwise_xor(mixed, lax.shift_right_logical(mixed, jnp.int32(16)))


def unit_value(index, stream, salt):
    upper = lax.shift_right_logical(hash_index(index, stream, salt), jnp.int32(9))
    return ((2 * upper + 1).astype(jnp.float32) * 2.0 ** (-24) - 1.0).astype(jnp.bfloat16)


def test_table(row_ids, col_ids, stride, stream, salt):
    return unit_value(row_ids[:, None] * stride + col_ids[None, :], stream, salt)


def shards_general(flow_field, test_streams, snapshot_ids):
    highest = lax.Precision.HIGHEST
    batches, local_snaps, variables, cells_x, cells_y, cells_z = flow_field.shape
    slabs_x = lax.axis_size("gx")
    total_x = cells_x * slabs_x
    total_z = cells_z * lax.axis_size("gz")
    total_q = variables * batches * local_snaps * lax.axis_size("vert")
    factor_stream = test_streams[0]
    core_stream = test_streams[1]
    rank_ids = jnp.arange(K, dtype=jnp.int32)
    sketch_ids = jnp.arange(S, dtype=jnp.int32)
    x_ids = lax.axis_index("gx") * cells_x + jnp.arange(cells_x, dtype=jnp.int32)
    y_ids = jnp.arange(cells_y, dtype=jnp.int32)
    z_ids = lax.axis_index("gz") * cells_z + jnp.arange(cells_z, dtype=jnp.int32)
    ax_tab = test_table(x_ids, rank_ids, K, factor_stream, 1).astype(jnp.float32)
    ay_low = test_table(y_ids, rank_ids, K, factor_stream, 2)
    az_low = test_table(z_ids, rank_ids, K, factor_stream, 3)
    ay_tab = ay_low.astype(jnp.float32)
    phy_low = test_table(sketch_ids, y_ids, cells_y, core_stream, 6)
    phz_low = test_table(sketch_ids, z_ids, total_z, core_stream, 7)

    def batch_terms(batch_idx):
        blocks = flow_field[batch_idx].reshape(-1, cells_x, cells_y, cells_z)
        pairs = blocks.shape[0]
        q_ids = (
            snapshot_ids[batch_idx][:, None] * variables
            + jnp.arange(variables, dtype=jnp.int32)[None, :]
        ).reshape(-1)
        aq_tab = test_table(q_ids, rank_ids, K, factor_stream, 4).astype(jnp.float32)
        phq_low = test_table(q_ids, jnp.arange(E, dtype=jnp.int32), E, core_stream, 8)
        rows_z = blocks.reshape(-1, cells_z)
        along_z = jnp.dot(rows_z, az_low, preferred_element_type=jnp.float32).reshape(
            pairs, cells_x, cells_y, K
        )
        along_y = jnp.einsum("qxyz,yk->qxzk", blocks, ay_low, preferred_element_type=jnp.float32)
        weights = aq_tab[:, None, :] * ax_tab[None, :, :]
        part_x = jnp.sum(
            jnp.sum(along_z * ay_tab[None, None, :, :], axis=2) * aq_tab[:, None, :], axis=0
        )
        part_y = jnp.sum(along_z * weights[:, :, None, :], axis=(0, 1))
        part_z = jnp.sum(along_y * weights[:, :, None, :], axis=(0, 1))
        first = jnp.dot(rows_z, phz_low.T, preferred_element_type=jnp.float32).reshape(
            pairs, cells_x, cells_y, S
        )
        second = jnp.einsum("qxyc,by->qxbc", first, phy_low.astype(jnp.float32), precision=highest)
        partial_core = jnp.einsum(
            "qxbc,qe->bcex", second, phq_low.astype(jnp.float32), precision=highest
        )
        return (part_x, part_y, part_z, partial_core.reshape(S * S, E, cells_x))

    def finish(part_x, part_y, part_z, partial_core):
        summed, sum_x = lax.psum((partial_core, part_x), ("gz", "vert"))
        phx_whole = test_table(
            sketch_ids, jnp.arange(total_x, dtype=jnp.int32), total_x, core_stream, 5
        ).astype(jnp.float32)
        core = jnp.einsum(
            "rex,ax->rea",
            lax.all_to_all(summed, "gx", split_axis=0, concat_axis=2, tiled=True),
            phx_whole,
            precision=highest,
        )
        sum_z = lax.psum_scatter(part_z, ("gx", "vert"), scatter_dimension=1, tiled=True)
        sum_y = lax.psum_scatter(part_y, ("gx", "gz", "vert"), scatter_dimension=0, tiled=True)
        return (sum_x, sum_y, sum_z, core)

    terms = [batch_terms(batch_idx) for batch_idx in range(batches)]
    totals = finish(terms[0][0], terms[0][1], terms[0][2], terms[0][3])
    for later in terms[1:]:
        latest = finish(later[0], later[1], later[2], later[3])
        totals = tuple((earlier + newer for earlier, newer in zip(totals, latest)))
    scale_x = 3.0**1.5 / math.sqrt(cells_y * total_z * total_q)
    scale_y = 3.0**1.5 / math.sqrt(total_x * total_z * total_q)
    scale_z = 3.0**1.5 / math.sqrt(total_x * cells_y * total_q)
    scale_core = 9.0 / math.sqrt(total_x * cells_y * total_z * total_q)
    return (totals[0] * scale_x, totals[1] * scale_y, totals[2] * scale_z, totals[3] * scale_core)


MESH = pl.DeviceIdType.MESH
PAD = 16


def iota(shape, dim):
    return lax.broadcasted_iota(jnp.int32, shape, dim)


def unit_f32(index, stream, salt):
    return unit_value(index, stream, salt).astype(jnp.float32)


def dot_f32(left, right):
    return jnp.dot(left, right, preferred_element_type=jnp.float32)


def dot_split(left, right):
    upper = left.astype(jnp.bfloat16)
    lower = (left - upper.astype(jnp.float32)).astype(jnp.bfloat16)
    return dot_f32(upper, right) + dot_f32(lower, right)


def sketch_kernel(
    sizes,
    scales,
    streams_hbm,
    snaps_hbm,
    flow_hbm,
    out_x,
    out_y,
    out_z,
    out_core,
    streams,
    snaps,
    flow,
    x_send,
    x_got,
    x_out,
    x_in,
    y_send,
    y_got,
    y_out,
    y_in,
    z_send,
    z_got,
    z_out,
    z_in,
    c_send,
    c_got,
    c_out,
    c_in,
    small_sem,
    load_sem,
    pair_send,
    pair_recv,
    x_ssem,
    x_rsem,
    y_ssem,
    y_rsem,
    c_ssem,
    c_rsem,
    z_ssem,
    z_rsem,
):
    slabs, zsplit, batches, local_snaps, variables, cells_y, cells_z = sizes
    scale_x, scale_y, scale_z, scale_core = scales
    pairs = batches * local_snaps
    total_q = pairs * variables
    chips = slabs * zsplit
    rows_y = cells_y // (2 * chips)
    rows_z = K // (2 * slabs)
    rows_m = S // slabs
    rows_c = slabs * PAD
    total_z = cells_z * zsplit
    gx = lax.axis_index("gx")
    gz = lax.axis_index("gz")
    vert = lax.axis_index("vert")
    other = 1 - vert
    offsets = [(dx, dz) for dx in range(slabs) for dz in range(zsplit)]
    far_first = sorted(range(1, chips), key=lambda i: -min(offsets[i][0], slabs - offsets[i][0]))

    def target(dx, dz):
        return {"gx": lax.rem(gx + dx, slabs), "gz": lax.rem(gz + dz, zsplit)}

    smalls = [
        pltpu.make_async_copy(streams_hbm, streams, small_sem.at[0]),
        pltpu.make_async_copy(snaps_hbm, snaps, small_sem.at[1]),
    ]
    loads = [
        pltpu.make_async_copy(
            flow_hbm.at[pl.ds(p * variables, variables)],
            flow.at[pl.ds(p * variables, variables)],
            load_sem.at[p],
        )
        for p in range(pairs)
    ]
    for load in smalls + loads:
        load.start()
    barrier = pltpu.get_barrier_semaphore()
    pl.semaphore_signal(barrier, inc=1, device_id={"vert": other}, device_id_type=MESH)
    for dx, dz in offsets[1:]:
        pl.semaphore_signal(barrier, inc=1, device_id=target(dx, dz), device_id_type=MESH)

    low = jnp.bfloat16
    select_at = iota((1, 640), 1)
    lane_m = select_at // S
    lane_n = select_at - lane_m * S
    spread = jnp.where((iota((K, 640), 0) & 63) == lane_n, 1.0, 0.0).astype(low)
    keep = (iota((rows_c, 640), 0) & (PAD - 1)) == lane_m
    for load in smalls:
        load.wait()
    fac = streams[0]
    cor = streams[1]

    def run_ids(q_index):
        ids = jnp.zeros(q_index.shape, jnp.int32)
        for q in range(total_q):
            p = q // variables
            run = snaps[p // local_snaps, p % local_snaps] * variables + q % variables
            ids = jnp.where(q_index == q, run, ids)
        return ids

    z_base = gz * cells_z
    ay_turned = unit_value(iota((K, cells_y), 1) * K + iota((K, cells_y), 0), fac, 2)
    m_row = iota((rows_c, cells_y), 0)
    m_ids = (m_row >> 4) * rows_m + (m_row & (PAD - 1))
    phy_tab = unit_value(m_ids * cells_y + iota((rows_c, cells_y), 1), cor, 6)
    turned = jnp.concatenate([ay_turned, phy_tab], axis=0)
    q_rows = -(-total_q // 8) * 8
    r_rows = run_ids(iota((q_rows, K), 0))
    aq_tab = unit_f32(r_rows * K + iota((q_rows, K), 1), fac, 4)
    phq_tab = [unit_f32(r_rows * E + e, cor, 8) for e in range(E)]
    aq_turned = unit_f32(run_ids(iota((1, K), 1)) * K + iota((K, K), 0), fac, 4)
    ax_turned = unit_f32(gx * K + iota((K, K), 0), fac, 1)
    weights = aq_turned * ax_turned

    deep = jnp.zeros((K, cells_z), jnp.float32)
    halves = [jnp.zeros((rows_c, cells_z), jnp.float32) for e in range(E)]
    waited = 0
    for first in range(0, total_q, 2):
        while waited * variables < min(first + 2, total_q):
            loads[waited].wait()
            waited += 1
        group = range(first, min(first + 2, total_q))
        both = dot_f32(turned, jnp.concatenate([flow[q] for q in group], axis=1))
        for i, q in enumerate(group):
            lanes = both[:, i * cells_z : (i + 1) * cells_z]
            deep = deep + lanes[:K] * weights[:, q : q + 1]
            for e in range(E):
                halves[e] = halves[e] + lanes[K:] * phq_tab[e][q : q + 1]
    for g in range(slabs):
        for v in range(2):
            at = (2 * g + v) * rows_z
            z_send[v, g] = deep[at : at + rows_z]

    pl.semaphore_wait(barrier, chips)

    def pair_copy(src, dst, which):
        return pltpu.make_async_remote_copy(
            src_ref=src,
            dst_ref=dst,
            send_sem=pair_send.at[which],
            recv_sem=pair_recv.at[which],
            device_id={"vert": other},
            device_id_type=MESH,
        )

    pair_z = pair_copy(z_send.at[other], z_got, 0)
    pair_z.start()
    lane = iota((cells_z, K), 1)
    phz_tab = unit_f32((lane & 63) * total_z + z_base + iota((cells_z, K), 0), cor, 7)
    core = None
    for e in range(E):
        right = jnp.where((lane >> 6) == e, phz_tab, 0.0).astype(low)
        part = dot_split(halves[e], right)
        core = part if core is None else core + part
    c_send[...] = core.reshape(slabs, PAD, K)
    pair_c = pair_copy(c_send, c_got, 1)
    pair_c.start()

    az_tab = unit_value(
        (z_base + iota((cells_z, K), 0)) * K + iota((cells_z, K), 1), fac, 3
    )
    ax_row = unit_f32(gx * K + iota((8, K), 1), fac, 1)[0:1]
    half = cells_y // 2
    pairs_y = []
    z_copies = []
    c_copies = [None] * chips
    x_row = jnp.zeros((1, K), jnp.float32)
    for h in range(2):
        wide = jnp.zeros((half, K), jnp.float32)
        for q in range(total_q):
            wide = wide + dot_f32(flow[q, h * half : (h + 1) * half], az_tab) * aq_tab[q : q + 1]
        y_index = h * half + iota((half, K), 0)
        ay_tab = unit_f32(y_index * K + iota((half, K), 1), fac, 2)
        x_row = x_row + jnp.sum(wide * ay_tab, axis=0, keepdims=True)
        wide = wide * ax_row
        for c in range(chips // 2):
            for v in range(2):
                at = (2 * c + v) * rows_y
                y_send[v, h * (chips // 2) + c] = wide[at : at + rows_y]
        at = pl.ds(h * (chips // 2), chips // 2)
        pair_y = pair_copy(y_send.at[other, at], y_got.at[at], 2 + h)
        pair_y.start()
        pairs_y.append(pair_y)
        if h == 0:
            pair_z.wait_recv()
            z_out[...] = z_send[vert] + z_got[...]
            for dx in range(1, slabs):
                to = lax.rem(gx + dx, slabs)
                copy = pltpu.make_async_remote_copy(
                    src_ref=z_out.at[to],
                    dst_ref=z_in.at[dx - 1],
                    send_sem=z_ssem.at[dx - 1],
                    recv_sem=z_rsem.at[dx - 1],
                    device_id={"gx": to},
                    device_id_type=MESH,
                )
                copy.start()
                z_copies.append(copy)
            pair_c.wait_recv()
            c_out[...] = c_send[...] + c_got[...]
            for i in far_first:
                dest = target(*offsets[i])
                copy = pltpu.make_async_remote_copy(
                    src_ref=c_out.at[dest["gx"]],
                    dst_ref=c_in.at[i - 1],
                    send_sem=c_ssem.at[i - 1],
                    recv_sem=c_rsem.at[i - 1],
                    device_id=dest,
                    device_id_type=MESH,
                )
                copy.start()
                c_copies[i] = copy
    x_send[...] = jnp.broadcast_to(x_row, x_send.shape)
    pair_x = pair_copy(x_send, x_got, 4)
    pair_x.start()

    for pair_y in pairs_y:
        pair_y.wait_recv()
    y_out[...] = y_send[vert] + y_got[...]
    y_copies = [None] * chips
    for i in far_first:
        dest = target(*offsets[i])
        copy = pltpu.make_async_remote_copy(
            src_ref=y_out.at[dest["gx"] * zsplit + dest["gz"]],
            dst_ref=y_in.at[i - 1],
            send_sem=y_ssem.at[i - 1],
            recv_sem=y_rsem.at[i - 1],
            device_id=dest,
            device_id_type=MESH,
        )
        copy.start()
        y_copies[i] = copy
    pair_x.wait_recv()
    x_out[...] = x_send[...] + x_got[...]
    x_copies = []
    for dz in range(1, zsplit):
        copy = pltpu.make_async_remote_copy(
            src_ref=x_out,
            dst_ref=x_in.at[dz - 1],
            send_sem=x_ssem.at[dz - 1],
            recv_sem=x_rsem.at[dz - 1],
            device_id={"gz": lax.rem(gz + dz, zsplit)},
            device_id_type=MESH,
        )
        copy.start()
        x_copies.append(copy)

    total = z_out[gx]
    for i, copy in enumerate(z_copies):
        copy.wait_recv()
        total = total + z_in[i]
    out_z[...] = total * scale_z
    slots = []
    for dx in range(slabs):
        total = c_out[gx] if dx == 0 else None
        for dz in range(zsplit):
            i = dx * zsplit + dz
            if i == 0:
                continue
            c_copies[i].wait_recv()
            total = c_in[i - 1] if total is None else total + c_in[i - 1]
        slots.append(total)
    core = jnp.concatenate(slots, axis=0) * scale_core
    upper = core.astype(low)
    lower = (core - upper.astype(jnp.float32)).astype(low)
    core_lane = iota((rows_c, K), 1) >> 6
    zero = jnp.zeros((rows_c, K), low)
    left = jnp.concatenate(
        [jnp.where(core_lane == e, part, zero) for e in range(E) for part in (upper, lower)],
        axis=0,
    )
    placed = dot_f32(left, spread)
    slot = iota((S, K), 1) >> 4
    x_ids = (gx - slot + 2 * slabs) & (slabs - 1)
    phx = unit_value(iota((S, K), 0) * slabs + x_ids, cor, 5)
    for e in range(E):
        at = 2 * e * rows_c
        right = jnp.concatenate(
            [
                jnp.where(keep, placed[at + s * rows_c : at + (s + 1) * rows_c], 0.0)
                for s in range(2)
            ],
            axis=0,
        ).astype(low)
        out_core[e] = dot_f32(phx, right)[:, : rows_m * S]

    total = x_out[...]
    for i, copy in enumerate(x_copies):
        copy.wait_recv()
        total = total + x_in[i]
    out_x[...] = total[0:1] * scale_x
    total = y_out[gx * zsplit + gz]
    for i in range(1, chips):
        y_copies[i].wait_recv()
        total = total + y_in[i - 1]
    out_y[...] = total * scale_y
    started = [pair_x, pair_z, pair_c] + pairs_y + x_copies + z_copies + c_copies[1:] + y_copies[1:]
    for copy in started:
        copy.wait_send()


def finish_kernel(*refs):
    count = len(refs) // 2
    for i in range(count):
        refs[count + i][...] = refs[i][...]


def shards_fused(sizes, flow_field, test_streams, snapshot_ids):
    slabs, zsplit, batches, local_snaps, variables, cells_y, cells_z = sizes
    pairs = batches * local_snaps
    chips = slabs * zsplit
    rows_y = cells_y // (2 * chips)
    rows_z = K // (2 * slabs)
    rows_m = S // slabs
    total_q = pairs * variables
    f32 = jnp.float32
    anywhere = pl.BlockSpec(memory_space=pl.ANY)
    vmem = pl.BlockSpec(memory_space=pltpu.VMEM)
    dma = pltpu.SemaphoreType.DMA
    total_z = cells_z * zsplit
    all_q = 2 * total_q
    scales = (
        3.0**1.5 / math.sqrt(cells_y * total_z * all_q),
        3.0**1.5 / math.sqrt(slabs * total_z * all_q),
        3.0**1.5 / math.sqrt(slabs * cells_y * all_q),
        9.0 / math.sqrt(slabs * cells_y * total_z * all_q),
    )
    outs = [
        jax.ShapeDtypeStruct((1, K), f32),
        jax.ShapeDtypeStruct((rows_y, K), f32),
        jax.ShapeDtypeStruct((rows_z, cells_z), f32),
        jax.ShapeDtypeStruct((E, S, rows_m * S), f32),
    ]
    parts = pl.pallas_call(
        functools.partial(sketch_kernel, sizes, scales),
        name="sketch",
        out_shape=outs,
        in_specs=[anywhere] * 3,
        out_specs=[vmem] * 4,
        scratch_shapes=[
            pltpu.SMEM(test_streams.shape, jnp.int32),
            pltpu.SMEM(snapshot_ids.shape, jnp.int32),
            pltpu.VMEM((total_q, cells_y, cells_z), jnp.bfloat16),
            pltpu.VMEM((8, K), f32),
            pltpu.VMEM((8, K), f32),
            pltpu.VMEM((8, K), f32),
            pltpu.VMEM((zsplit - 1, 8, K), f32),
            pltpu.VMEM((2, chips, rows_y, K), f32),
            pltpu.VMEM((chips, rows_y, K), f32),
            pltpu.VMEM((chips, rows_y, K), f32),
            pltpu.VMEM((chips - 1, rows_y, K), f32),
            pltpu.VMEM((2, slabs, rows_z, cells_z), f32),
            pltpu.VMEM((slabs, rows_z, cells_z), f32),
            pltpu.VMEM((slabs, rows_z, cells_z), f32),
            pltpu.VMEM((slabs - 1, rows_z, cells_z), f32),
            pltpu.VMEM((slabs, PAD, K), f32),
            pltpu.VMEM((slabs, PAD, K), f32),
            pltpu.VMEM((slabs, PAD, K), f32),
            pltpu.VMEM((chips - 1, PAD, K), f32),
            dma((2,)),
            dma((pairs,)),
            dma((5,)),
            dma((5,)),
            dma((zsplit - 1,)),
            dma((zsplit - 1,)),
            dma((chips - 1,)),
            dma((chips - 1,)),
            dma((chips - 1,)),
            dma((chips - 1,)),
            dma((slabs - 1,)),
            dma((slabs - 1,)),
        ],
        compiler_params=pltpu.CompilerParams(
            collective_id=0, has_side_effects=True, vmem_limit_bytes=63 * 2**20
        ),
    )(test_streams, snapshot_ids, flow_field.reshape(total_q, cells_y, cells_z))
    out_x, out_y, out_z, out_core = pl.pallas_call(
        finish_kernel,
        name="finish",
        out_shape=outs,
        in_specs=[vmem] * 4,
        out_specs=[vmem] * 4,
        compiler_params=pltpu.CompilerParams(vmem_limit_bytes=63 * 2**20),
    )(*parts)
    return (out_x, out_y, out_z.T, jnp.transpose(out_core, (2, 0, 1)))


def shards(flow_field, test_streams, snapshot_ids):
    batches, local_snaps, variables, cells_x, cells_y, cells_z = flow_field.shape
    slabs = lax.axis_size("gx")
    zsplit = lax.axis_size("gz")
    fits = (
        lax.axis_size("vert") == 2
        and cells_x == 1
        and cells_z == K
        and cells_y % (16 * slabs * zsplit) == 0
        and slabs == 4
        and zsplit > 1
        and batches * local_snaps * variables <= K
    )
    if not fits:
        return shards_general(flow_field, test_streams, snapshot_ids)
    sizes = (slabs, zsplit, batches, local_snaps, variables, cells_y, cells_z)
    return shards_fused(sizes, flow_field, test_streams, snapshot_ids)


def solution(mesh):
    in_specs = (P("groups", "vert", None, "gx", None, "gz"), P("groups"), P("groups", "vert"))
    out_specs = (
        P(("groups", "gx"), None),
        P(("groups", "gx", "gz", "vert"), None),
        P(("groups", "gz"), ("gx", "vert")),
        P(("groups", "gx"), None, None),
    )
    return jax.shard_map(shards, mesh=mesh, in_specs=in_specs, out_specs=out_specs, check_vma=False)
```

profile of v0, /device:TPU:0, one launch (start us, length us, event | category | flops | bytes accessed | tf_op | source)
XLA Modules:
  0.0 16.2 jit_solution(13691725669012650903)
XLA Ops:
  0.6 13.9 %sketch.1 = (f32[1,128]{1,0:T(1,128)}, f32[16,128]{1,0:T(8,128)}, f32[16,128]{1,0:T(8,128)}, f32[2,48,576]{2,1,0:T(8,128)}) custom-call(s32[2]{0:T(128)} %streams_hbm.1, s32[2,2]{1,0:T(2,128)} %snaps_hbm.1, bf16[20,256,128]{2,1,0:T(8,128)(2,1)} %bitcast.3), custom_call_target="tpu_custom_call" | custom-call | tf_op jit(solution)/shard_map/sketch/pallas_call | solution.py:466
  14.5 1.7 %finish.1 = (f32[1,128]{1,0:T(1,128)}, f32[16,128]{1,0:T(8,128)}, f32[16,128]{1,0:T(8,128)}, f32[2,48,576]{2,1,0:T(8,128)}) custom-call(f32[1,128]{1,0:T(1,128)} %get-tuple-element.12.refs_0_, f32[16,128]{1,0:T(8,128)} %get-tuple-element.13.refs_1_, f32[16,128]{1,0:T(8,128)} %get-tuple-element.14.refs_2_, f32[2,48,576]{2,1,0:T(8,128)} %get-tuple-element.15.refs_3_), custom_call_target="tpu_custom_call" | custom-call | tf_op jit(solution)/shard_map/finish/pallas_call | solution.py:509
where the time goes:
time: 16.4 us; the launch traced here: 16.2 us
  Pallas kernels  15.6 us (95%)
  between operations  0.64 us (4%)
    pallas_call x1, Pallas kernels, shards_fused(): pl.pallas_call(functools.partial(sketch_kernel, sizes, scales), name='ske...  13.9 us
    pallas_call x1, Pallas kernels, shards_fused(): pl.pallas_call(finish_kernel, name='finish', out_shape=outs, in_specs=[vm...  1.7 us

commit v1 on v0

--- a/solution.py
+++ b/solution.py
@@ -143,10 +143,6 @@
     streams,
     snaps,
     flow,
-    x_send,
-    x_got,
-    x_out,
-    x_in,
     y_send,
     y_got,
     y_out,
@@ -163,8 +159,6 @@
     load_sem,
     pair_send,
     pair_recv,
-    x_ssem,
-    x_rsem,
     y_ssem,
     y_rsem,
     c_ssem,
@@ -242,7 +236,9 @@
     phq_tab = [unit_f32(r_rows * E + e, cor, 8) for e in range(E)]
     aq_turned = unit_f32(run_ids(iota((1, K), 1)) * K + iota((K, K), 0), fac, 4)
     ax_turned = unit_f32(gx * K + iota((K, K), 0), fac, 1)
-    weights = aq_turned * ax_turned
+    az_tab = unit_value(
+        (z_base + iota((cells_z, K), 0)) * K + iota((cells_z, K), 1), fac, 3
+    )
 
     deep = jnp.zeros((K, cells_z), jnp.float32)
     halves = [jnp.zeros((rows_c, cells_z), jnp.float32) for e in range(E)]
@@ -252,16 +248,16 @@
             loads[waited].wait()
             waited += 1
         group = range(first, min(first + 2, total_q))
-        both = dot_f32(turned, jnp.concatenate([flow[q] for q in group], axis=1))
+        both = dot_f32(turned, jnp.concatenate([flow[q].reshape(cells_y, cells_z) for q in group], axis=1))
         for i, q in enumerate(group):
             lanes = both[:, i * cells_z : (i + 1) * cells_z]
-            deep = deep + lanes[:K] * weights[:, q : q + 1]
+            deep = deep + lanes[:K] * aq_turned[:, q : q + 1]
             for e in range(E):
                 halves[e] = halves[e] + lanes[K:] * phq_tab[e][q : q + 1]
     for g in range(slabs):
         for v in range(2):
             at = (2 * g + v) * rows_z
-            z_send[v, g] = deep[at : at + rows_z]
+            z_send[v, g] = deep[at : at + rows_z] * ax_turned[at : at + rows_z]
 
     pl.semaphore_wait(barrier, chips)
 
@@ -284,35 +280,25 @@
         right = jnp.where((lane >> 6) == e, phz_tab, 0.0).astype(low)
         part = dot_split(halves[e], right)
         core = part if core is None else core + part
+    x_row = jnp.sum(deep.T * az_tab.astype(jnp.float32), axis=0, keepdims=True)
+    core = jnp.where((iota((rows_c, K), 0) & (PAD - 1)) == rows_m, x_row, core)
     c_send[...] = core.reshape(slabs, PAD, K)
     pair_c = pair_copy(c_send, c_got, 1)
     pair_c.start()
 
-    az_tab = unit_value(
-        (z_base + iota((cells_z, K), 0)) * K + iota((cells_z, K), 1), fac, 3
-    )
     ax_row = unit_f32(gx * K + iota((8, K), 1), fac, 1)[0:1]
-    half = cells_y // 2
-    pairs_y = []
     z_copies = []
     c_copies = [None] * chips
-    x_row = jnp.zeros((1, K), jnp.float32)
-    for h in range(2):
-        wide = jnp.zeros((half, K), jnp.float32)
+    for h, side in enumerate((other, vert)):
+        wide = jnp.zeros((chips * rows_y, K), jnp.float32)
         for q in range(total_q):
-            wide = wide + dot_f32(flow[q, h * half : (h + 1) * half], az_tab) * aq_tab[q : q + 1]
-        y_index = h * half + iota((half, K), 0)
-        ay_tab = unit_f32(y_index * K + iota((half, K), 1), fac, 2)
-        x_row = x_row + jnp.sum(wide * ay_tab, axis=0, keepdims=True)
-        wide = wide * ax_row
-        for c in range(chips // 2):
-            for v in range(2):
-                at = (2 * c + v) * rows_y
-                y_send[v, h * (chips // 2) + c] = wide[at : at + rows_y]
-        at = pl.ds(h * (chips // 2), chips // 2)
-        pair_y = pair_copy(y_send.at[other, at], y_got.at[at], 2 + h)
-        pair_y.start()
-        pairs_y.append(pair_y)
+            rows = flow[q, :, side].reshape(chips * rows_y, cells_z)
+            wide = wide + dot_f32(rows, az_tab) * aq_tab[q : q + 1]
+        wide = (wide * ax_row).reshape(chips, rows_y, K)
+        if h == 0:
+            y_send[...] = wide
+            pair_y = pair_copy(y_send, y_got, 2)
+            pair_y.start()
         if h == 0:
             pair_z.wait_recv()
             z_out[...] = z_send[vert] + z_got[...]
@@ -342,13 +328,8 @@
                 )
                 copy.start()
                 c_copies[i] = copy
-    x_send[...] = jnp.broadcast_to(x_row, x_send.shape)
-    pair_x = pair_copy(x_send, x_got, 4)
-    pair_x.start()
-
-    for pair_y in pairs_y:
-        pair_y.wait_recv()
-    y_out[...] = y_send[vert] + y_got[...]
+    pair_y.wait_recv()
+    y_out[...] = wide + y_got[...]
     y_copies = [None] * chips
     for i in far_first:
         dest = target(*offsets[i])
@@ -362,21 +343,6 @@
         )
         copy.start()
         y_copies[i] = copy
-    pair_x.wait_recv()
-    x_out[...] = x_send[...] + x_got[...]
-    x_copies = []
-    for dz in range(1, zsplit):
-        copy = pltpu.make_async_remote_copy(
-            src_ref=x_out,
-            dst_ref=x_in.at[dz - 1],
-            send_sem=x_ssem.at[dz - 1],
-            recv_sem=x_rsem.at[dz - 1],
-            device_id={"gz": lax.rem(gz + dz, zsplit)},
-            device_id_type=MESH,
-        )
-        copy.start()
-        x_copies.append(copy)
-
     total = z_out[gx]
     for i, copy in enumerate(z_copies):
         copy.wait_recv()
@@ -392,6 +358,7 @@
             c_copies[i].wait_recv()
             total = c_in[i - 1] if total is None else total + c_in[i - 1]
         slots.append(total)
+    out_x[...] = slots[0][rows_m : rows_m + 1] * scale_x
     core = jnp.concatenate(slots, axis=0) * scale_core
     upper = core.astype(low)
     lower = (core - upper.astype(jnp.float32)).astype(low)
@@ -416,17 +383,12 @@
         ).astype(low)
         out_core[e] = dot_f32(phx, right)[:, : rows_m * S]
 
-    total = x_out[...]
-    for i, copy in enumerate(x_copies):
-        copy.wait_recv()
-        total = total + x_in[i]
-    out_x[...] = total[0:1] * scale_x
     total = y_out[gx * zsplit + gz]
     for i in range(1, chips):
         y_copies[i].wait_recv()
         total = total + y_in[i - 1]
     out_y[...] = total * scale_y
-    started = [pair_x, pair_z, pair_c] + pairs_y + x_copies + z_copies + c_copies[1:] + y_copies[1:]
+    started = [pair_z, pair_c, pair_y] + z_copies + c_copies[1:] + y_copies[1:]
     for copy in started:
         copy.wait_send()
 
@@ -472,12 +434,8 @@
         scratch_shapes=[
             pltpu.SMEM(test_streams.shape, jnp.int32),
             pltpu.SMEM(snapshot_ids.shape, jnp.int32),
-            pltpu.VMEM((total_q, cells_y, cells_z), jnp.bfloat16),
-            pltpu.VMEM((8, K), f32),
-            pltpu.VMEM((8, K), f32),
-            pltpu.VMEM((8, K), f32),
-            pltpu.VMEM((zsplit - 1, 8, K), f32),
-            pltpu.VMEM((2, chips, rows_y, K), f32),
+            pltpu.VMEM((total_q, chips, 2, rows_y, cells_z), jnp.bfloat16),
+            pltpu.VMEM((chips, rows_y, K), f32),
             pltpu.VMEM((chips, rows_y, K), f32),
             pltpu.VMEM((chips, rows_y, K), f32),
             pltpu.VMEM((chips - 1, rows_y, K), f32),
@@ -491,10 +449,8 @@
             pltpu.VMEM((chips - 1, PAD, K), f32),
             dma((2,)),
             dma((pairs,)),
-            dma((5,)),
-            dma((5,)),
-            dma((zsplit - 1,)),
-            dma((zsplit - 1,)),
+            dma((3,)),
+            dma((3,)),
             dma((chips - 1,)),
             dma((chips - 1,)),
             dma((chips - 1,)),
@@ -505,7 +461,7 @@
         compiler_params=pltpu.CompilerParams(
             collective_id=0, has_side_effects=True, vmem_limit_bytes=63 * 2**20
         ),
-    )(test_streams, snapshot_ids, flow_field.reshape(total_q, cells_y, cells_z))
+    )(test_streams, snapshot_ids, flow_field.reshape(total_q, chips, 2, rows_y, cells_z))
     out_x, out_y, out_z, out_core = pl.pallas_call(
         finish_kernel,
         name="finish",
@@ -528,6 +484,7 @@
         and cells_y % (16 * slabs * zsplit) == 0
         and slabs == 4
         and zsplit > 1
+        and cells_y % (32 * slabs * zsplit) == 0
         and batches * local_snaps * variables <= K
     )
     if not fits:

time: 16.4 us -> 16.2 us (0.988)
  Pallas kernels: 15.6 us -> 15.4 us
    pallas_call x1, Pallas kernels: 13.9 us -> 13.7 us  [shards_fused(): pl.pallas_call(functools.partial(sketch_kernel, sizes, scales), name='ske...]
where the time goes in v1:
time: 16.2 us; the launch traced here: 16 us
  Pallas kernels  15.4 us (95%)
  between operations  0.64 us (4%)
    pallas_call x1, Pallas kernels, shards_fused(): pl.pallas_call(functools.partial(sketch_kernel, sizes, scales), name='ske...  13.7 us
    pallas_call x1, Pallas kernels, shards_fused(): pl.pallas_call(finish_kernel, name='finish', out_shape=outs, in_specs=[vm...  1.7 us

profile of v1, /device:TPU:0, one launch (start us, length us, event | category | flops | bytes accessed | tf_op | source)
XLA Modules:
  0.0 16.0 jit_solution(6809317870834288357)
XLA Ops:
  0.6 13.7 %sketch.1 = (f32[1,128]{1,0:T(1,128)}, f32[16,128]{1,0:T(8,128)}, f32[16,128]{1,0:T(8,128)}, f32[2,48,576]{2,1,0:T(8,128)}) custom-call(s32[2]{0:T(128)} %streams_hbm.1, s32[2,2]{1,0:T(2,128)} %snaps_hbm.1, bf16[20,8,2,16,128]{4,3,2,1,0:T(8,128)(2,1)} %bitcast.3), custom_call_target="tpu_custom_call" | custom-call | tf_op jit(solution)/shard_map/sketch/pallas_call | solution.py:428
  14.3 1.7 %finish.1 = (f32[1,128]{1,0:T(1,128)}, f32[16,128]{1,0:T(8,128)}, f32[16,128]{1,0:T(8,128)}, f32[2,48,576]{2,1,0:T(8,128)}) custom-call(f32[1,128]{1,0:T(1,128)} %get-tuple-element.12.refs_0_, f32[16,128]{1,0:T(8,128)} %get-tuple-element.13.refs_1_, f32[16,128]{1,0:T(8,128)} %get-tuple-element.14.refs_2_, f32[2,48,576]{2,1,0:T(8,128)} %get-tuple-element.15.refs_3_), custom_call_target="tpu_custom_call" | custom-call | tf_op jit(solution)/shard_map/finish/pallas_call | solution.py:465

commit v2 on v1

--- a/solution.py
+++ b/solution.py
@@ -282,7 +282,8 @@
         core = part if core is None else core + part
     x_row = jnp.sum(deep.T * az_tab.astype(jnp.float32), axis=0, keepdims=True)
     core = jnp.where((iota((rows_c, K), 0) & (PAD - 1)) == rows_m, x_row, core)
-    c_send[...] = core.reshape(slabs, PAD, K)
+    for g in range(slabs):
+        c_send[g] = core[g * PAD : g * PAD + rows_m + 1]
     pair_c = pair_copy(c_send, c_got, 1)
     pair_c.start()
 
@@ -357,8 +358,9 @@
                 continue
             c_copies[i].wait_recv()
             total = c_in[i - 1] if total is None else total + c_in[i - 1]
-        slots.append(total)
-    out_x[...] = slots[0][rows_m : rows_m + 1] * scale_x
+        if dx == 0:
+            out_x[...] = total[rows_m : rows_m + 1] * scale_x
+        slots.append(jnp.concatenate([total, jnp.zeros((PAD - rows_m - 1, K), jnp.float32)], axis=0))
     core = jnp.concatenate(slots, axis=0) * scale_core
     upper = core.astype(low)
     lower = (core - upper.astype(jnp.float32)).astype(low)
@@ -443,10 +445,10 @@
             pltpu.VMEM((slabs, rows_z, cells_z), f32),
             pltpu.VMEM((slabs, rows_z, cells_z), f32),
             pltpu.VMEM((slabs - 1, rows_z, cells_z), f32),
-            pltpu.VMEM((slabs, PAD, K), f32),
-            pltpu.VMEM((slabs, PAD, K), f32),
-            pltpu.VMEM((slabs, PAD, K), f32),
-            pltpu.VMEM((chips - 1, PAD, K), f32),
+            pltpu.VMEM((slabs, rows_m + 1, K), f32),
+            pltpu.VMEM((slabs, rows_m + 1, K), f32),
+            pltpu.VMEM((slabs, rows_m + 1, K), f32),
+            pltpu.VMEM((chips - 1, rows_m + 1, K), f32),
             dma((2,)),
             dma((pairs,)),
             dma((3,)),

time: 16.2 us -> 16 us (0.988)
  Pallas kernels: 15.4 us -> 15.2 us
    pallas_call x1, Pallas kernels: 13.7 us -> 13.5 us  [shards_fused(): pl.pallas_call(functools.partial(sketch_kernel, sizes, scales), name='ske...]
where the time goes in v2:
time: 16 us; the launch traced here: 15.8 us
  Pallas kernels  15.2 us (95%)
  between operations  0.64 us (4%)
    pallas_call x1, Pallas kernels, shards_fused(): pl.pallas_call(functools.partial(sketch_kernel, sizes, scales), name='ske...  13.5 us
    pallas_call x1, Pallas kernels, shards_fused(): pl.pallas_call(finish_kernel, name='finish', out_shape=outs, in_specs=[vm...  1.7 us

profile of v2, /device:TPU:0, one launch (start us, length us, event | category | flops | bytes accessed | tf_op | source)
XLA Modules:
  0.0 15.8 jit_solution(10743273247465647897)
XLA Ops:
  0.6 13.5 %sketch.1 = (f32[1,128]{1,0:T(1,128)}, f32[16,128]{1,0:T(8,128)}, f32[16,128]{1,0:T(8,128)}, f32[2,48,576]{2,1,0:T(8,128)}) custom-call(s32[2]{0:T(128)} %streams_hbm.1, s32[2,2]{1,0:T(2,128)} %snaps_hbm.1, bf16[20,8,2,16,128]{4,3,2,1,0:T(8,128)(2,1)} %bitcast.3), custom_call_target="tpu_custom_call" | custom-call | tf_op jit(solution)/shard_map/sketch/pallas_call | solution.py:430
  14.1 1.7 %finish.1 = (f32[1,128]{1,0:T(1,128)}, f32[16,128]{1,0:T(8,128)}, f32[16,128]{1,0:T(8,128)}, f32[2,48,576]{2,1,0:T(8,128)}) custom-call(f32[1,128]{1,0:T(1,128)} %get-tuple-element.12.refs_0_, f32[16,128]{1,0:T(8,128)} %get-tuple-element.13.refs_1_, f32[16,128]{1,0:T(8,128)} %get-tuple-element.14.refs_2_, f32[2,48,576]{2,1,0:T(8,128)} %get-tuple-element.15.refs_3_), custom_call_target="tpu_custom_call" | custom-call | tf_op jit(solution)/shard_map/finish/pallas_call | solution.py:467
